TPU v7x, 32 devices: a whole 2x2x4 slice. The times are simulated.
32 devices in a mesh: tm: 4 (over y, core), height: 4 (over z), dp: 2 (over x).
Axes of the slice: x: 2, y: 2, z: 4, core: 2. Of those that a mesh axis runs over, the one named last changes fastest.
Arguments:
- queries: bfloat16 [4, 4, 4, 1, 192, 128], P('tm', 'height', 'dp'), may hold values from -4.5 to 4.5
- keys: bfloat16 [4, 4, 4, 1, 192, 128], P('tm', 'height', 'dp'), may hold values from -4.5 to 4.5
- values: bfloat16 [4, 4, 4, 1, 192, 128], P('tm', 'height', 'dp'), may hold values from -6 to 6
- grad_out: bfloat16 [4, 4, 4, 1, 192, 128], P('tm', 'height', 'dp'), may hold values from -24 to 24
- attn_out: bfloat16 [4, 4, 4, 1, 192, 128], P('tm', 'height', 'dp'), may hold values from -1.796875 to 1.796875
- window_mask: int32 [4, 4, 1, 27], P('tm', 'height'), may hold values 0 or 1
Outputs:
- grad_queries: bfloat16 [4, 4, 4, 1, 192, 128], P('tm', 'height', 'dp')
- grad_keys: bfloat16 [4, 4, 4, 1, 192, 128], P('tm', 'height', 'dp')
- grad_values: bfloat16 [4, 4, 4, 1, 192, 128], P('tm', 'height', 'dp')
All inputs are finite; a program needn't handle non-finite values. No bound on the sum of `window_mask` on one device may be relied on, other than what follows from the above.
Results may differ from a plain program's by a relative error of at most 0.009.
Values may be sent and summed in bfloat16 or wider, within the bound.
No kernel may reach another device: no remote copies, remote signals or barrier semaphores. Data moves between devices by JAX's collectives and lax.ppermute only.
A program may use at most 64 MiB of HBM per device.

v0:
```python
import jax
import jax.numpy as jnp
from jax import lax
from jax.sharding import PartitionSpec as P


def with_halo(value, sides, width):
    for axis, dim in sides:
        size, length = (lax.axis_size(axis), value.shape[dim])
        up = [(i, (i + 1) % size) for i in range(size - 1)]
        down = [(j, i) for i, j in up]
        last = lax.slice_in_dim(value, length - width, length, axis=dim)
        initial = lax.slice_in_dim(value, 0, width, axis=dim)
        before = lax.ppermute(last, axis, up)
        after = lax.ppermute(initial, axis, down)
        value = jnp.concatenate([before, value, after], axis=dim)
    return value


def from_behind(block, axis, distance):
    devices = range(lax.axis_size(axis))
    route = [(i - distance, i) for i in devices if i - distance in devices]
    return lax.ppermute(block, axis, route)


def tile_scores(query_rows, key_rows, score_scale):
    return (
        jnp.einsum("hwqd,hwkd->hwqk", query_rows, key_rows, preferred_element_type=jnp.float32)
        * score_scale
    )


def probs_and_grads(
    query_rows, grad_rows, log_rows, delta_part, key_rows, value_rows, allowed, score_scale
):
    scores = tile_scores(query_rows, key_rows, score_scale)
    prob_weights = jnp.where(
        allowed[None, :, None, None], jnp.exp(scores - log_rows[..., None]), 0.0
    )
    prob_grads = jnp.einsum(
        "hwqd,hwkd->hwqk", grad_rows, value_rows, preferred_element_type=jnp.float32
    )
    score_grads = (prob_weights * (prob_grads - delta_part[..., None]) * score_scale).astype(
        jnp.bfloat16
    )
    return (prob_weights.astype(jnp.bfloat16), score_grads)


def pair_terms(probs_low, score_grads, query_rows, grad_rows):
    key_part = jnp.einsum(
        "hwqk,hwqd->hwkd", score_grads, query_rows, preferred_element_type=jnp.float32
    )
    value_part = jnp.einsum(
        "hwqk,hwqd->hwkd", probs_low, grad_rows, preferred_element_type=jnp.float32
    )
    return jnp.stack([key_part, value_part])


def body(queries, keys, values, grad_out, attn_out, window_mask):
    head_size = queries.shape[-1]
    score_scale = head_size ** (-0.5)
    tiles_wide = queries.shape[3]
    video_time = lax.axis_size("tm")
    video_height = lax.axis_size("height")
    time_local = lax.axis_index("tm") % video_time
    height_local = lax.axis_index("height") % video_height
    query_here = queries[0, 0]
    grads_here = grad_out[0, 0]
    output_here = attn_out[0, 0]
    mask_here = window_mask[0, 0]
    stacked_kv = jnp.stack([keys, values], axis=2)
    kv_block = with_halo(stacked_kv, (("tm", 0), ("height", 1)), 1)

    def inside(step_time, step_height):
        time_at = time_local + step_time - 1
        height_at = height_local + step_height - 1
        return (
            (time_at >= 0) & (time_at < video_time) & (height_at >= 0) & (height_at < video_height)
        )

    def width_span(step_width):
        return (max(0, 1 - step_width), min(tiles_wide, tiles_wide + 1 - step_width))

    def allowed_tiles(mask_rows, step_time, step_height, window_slot):
        picked = mask_rows != 0
        if window_slot == 13:
            picked = jnp.ones_like(picked)
        return picked & inside(step_time, step_height)

    offsets = [
        (step_time, step_height, step_width)
        for step_time in range(3)
        for step_height in range(3)
        for step_width in range(3)
        if width_span(step_width)[0] < width_span(step_width)[1]
    ]
    rows_shape = query_here.shape[:-1]
    running_top = jnp.full(rows_shape, -1e30, jnp.float32)
    running_total = jnp.zeros(rows_shape, jnp.float32)
    for step_time, step_height, step_width in offsets:
        start_at, stop_at = width_span(step_width)
        window_slot = 9 * step_time + 3 * step_height + step_width
        allowed = allowed_tiles(
            mask_here[start_at:stop_at, window_slot], step_time, step_height, window_slot
        )
        key_rows = kv_block[step_time, step_height, 0]

        def update(carried):
            top_all, total_all = carried
            scores = jnp.where(
                allowed[None, :, None, None], tile_scores(query_here, key_rows, score_scale), -1e30
            )
            new_top = jnp.maximum(top_all, scores.max(-1))
            new_total = total_all * jnp.exp(top_all - new_top) + jnp.exp(
                scores - new_top[..., None]
            ).sum(-1)
            return (
                top_all.at[:, start_at:stop_at].set(new_top),
                total_all.at[:, start_at:stop_at].set(new_total),
            )

        running_top, running_total = lax.cond(
            jnp.any(allowed), update, lambda carried: carried, (running_top, running_total)
        )
    log_total = running_top + jnp.log(running_total)
    delta_rows = jnp.sum(grads_here.astype(jnp.float32) * output_here.astype(jnp.float32), axis=-1)
    row_grads = jnp.zeros(query_here.shape, jnp.float32)
    columns = []
    for local_step_time in range(3):
        column_line = []
        for step_height in range(3):
            column = jnp.zeros((2,) + query_here.shape, jnp.float32)
            for step_width in range(3):
                local_start_at, local_stop_at = width_span(step_width)
                if local_start_at >= local_stop_at:
                    continue
                window_slot = 9 * local_step_time + 3 * step_height + step_width
                local_allowed = allowed_tiles(
                    mask_here[local_start_at:local_stop_at, window_slot],
                    local_step_time,
                    step_height,
                    window_slot,
                )
                kv_rows = kv_block[local_step_time, step_height]
                pair_count = local_stop_at - local_start_at
                row_shape = (query_here.shape[0], pair_count) + query_here.shape[2:]

                def active(unused):
                    probs_low, score_grads = probs_and_grads(
                        query_here,
                        grads_here,
                        log_total,
                        delta_rows,
                        kv_rows[0],
                        kv_rows[1],
                        local_allowed,
                        score_scale,
                    )
                    row_part = jnp.einsum(
                        "hwqk,hwkd->hwqd",
                        score_grads,
                        kv_rows[0],
                        preferred_element_type=jnp.float32,
                    )
                    return (row_part, pair_terms(probs_low, score_grads, query_here, grads_here))

                def silent(unused):
                    return (
                        jnp.zeros(row_shape, jnp.float32),
                        jnp.zeros((2,) + row_shape, jnp.float32),
                    )

                result = lax.cond(jnp.any(local_allowed), active, silent, 0)
                row_part, key_part = result
                column = column.at[
                    :, :, local_start_at + step_width - 1 : local_stop_at + step_width - 1
                ].add(key_part)
                row_grads = row_grads.at[:, local_start_at:local_stop_at].add(row_part)
            column_line.append(column.astype(jnp.bfloat16))
        columns.append(column_line)
    row_grads, columns = (row_grads, columns)
    columns = lax.optimization_barrier(columns)
    through_height = [columns[step_time][1].astype(jnp.float32) for step_time in range(3)]
    for shift_by, picked_side in ((1, 2), (-1, 0)):
        arrived = from_behind(
            jnp.stack([columns[step_time][picked_side] for step_time in range(3)]),
            "height",
            shift_by,
        )
        through_height = [
            through_height[step_time] + arrived[step_time].astype(jnp.float32)
            for step_time in range(3)
        ]
    key_grads = through_height[1]
    for shift_by, picked_side in ((1, 2), (-1, 0)):
        key_grads = key_grads + from_behind(
            through_height[picked_side].astype(jnp.bfloat16), "tm", shift_by
        ).astype(jnp.float32)
    grad_queries = row_grads.astype(jnp.bfloat16)[None, None]
    grad_keys = key_grads[0].astype(jnp.bfloat16)[None, None]
    grad_values = key_grads[1].astype(jnp.bfloat16)[None, None]
    return (grad_queries, grad_keys, grad_values)


def solution(mesh):
    placed = (
        P("tm", "height", "dp", None, None, None),
        P("tm", "height", "dp", None, None, None),
        P("tm", "height", "dp", None, None, None),
        P("tm", "height", "dp", None, None, None),
        P("tm", "height", "dp", None, None, None),
        P("tm", "height", None, None),
    )
    return jax.shard_map(
        body,
        mesh=mesh,
        in_specs=placed,
        out_specs=(
            P("tm", "height", "dp", None, None, None),
            P("tm", "height", "dp", None, None, None),
            P("tm", "height", "dp", None, None, None),
        ),
        check_vma=False,
    )
```

profile of v0, /device:TPU:1, one launch (start us, length us, event | category | flops | bytes accessed | tf_op | source)
XLA Modules:
  0.0 77.0 jit_solution(16378400197581117586)
XLA Ops:
  0.7 1.0 %pad_maximum_fusion.12 = bf16[1,1,2,2,1,192,128]{6,5,3,4,2,1,0:T(8,128)(2,1)S(1)} fusion(bf16[1,1,1,2,1,192,128]{6,5,3,4,2,1,0:T(8,128)(2,1)} %bitcast.547, bf16[1,1,1,2,1,192,128]{6,5,3,4,2,1,0:T(8,128)(2,1)} %bitcast.539), kind=kLoop, calls=%fused_computation.312 | loop fusion | flops 98304 | bytes 393216 | tf_op jit(solution)/shard_map/stack | solution.py:71
  1.7 4.5 %collective-permute-start = (bf16[1,1,2,2,1,192,128]{6,5,3,4,2,1,0:T(8,128)(2,1)S(1)}, bf16[1,1,2,2,1,192,128]{6,5,3,4,2,1,0:T(8,128)(2,1)S(1)}, u32[]{:S(2)}, u32[]{:S(2)}) collective-permute-start(bf16[1,1,2,2,1,192,128]{6,5,3,4,2,1,0:T(8,128)(2,1)S(1)} %pad_maximum_fusion.12), channel_id=1, source_target_pairs={{0,8},{8,16},{16,24},{1,9},{9,17},{17,25},{2,10},{10,18},{18,26},{... | collective-permute-start | bytes 589832 | tf_op jit(solution)/shard_map/ppermute | solution.py:14
  6.2 1.9 %collective-permute-start.1 = (bf16[1,1,2,2,1,192,128]{6,5,3,4,2,1,0:T(8,128)(2,1)S(1)}, bf16[1,1,2,2,1,192,128]{6,5,3,4,2,1,0:T(8,128)(2,1)S(1)}, u32[]{:S(2)}, u32[]{:S(2)}) collective-permute-start(bf16[1,1,2,2,1,192,128]{6,5,3,4,2,1,0:T(8,128)(2,1)S(1)} %pad_maximum_fusion.12), channel_id=1, source_target_pairs={{8,0},{16,8},{24,16},{9,1},{17,9},{25,17},{10,2},{18,10},{26,18},{... | collective-permute-start | bytes 589832 | tf_op jit(solution)/shard_map/ppermute | solution.py:15
  8.1 0.7 collective-permute-done
  8.8 4.4 %collective-permute-done.1 = bf16[1,1,2,2,1,192,128]{6,5,3,4,2,1,0:T(8,128)(2,1)S(1)} collective-permute-done((bf16[1,1,2,2,1,192,128]{6,5,3,4,2,1,0:T(8,128)(2,1)S(1)}, bf16[1,1,2,2,1,192,128]{6,5,3,4,2,1,0:T(8,128)(2,1)S(1)}, u32[]{:S(2)}, u32[]{:S(2)}) %collective-permute-start.1) | collective-permute-done | bytes 196640 | tf_op jit(solution)/shard_map/ppermute | solution.py:15
  13.3 3.2 %collective-permute-start.2 = (bf16[3,1,2,2,1,192,128]{6,5,3,4,2,1,0:T(8,128)(2,1)S(1)}, bf16[3,1,2,2,1,192,128]{6,5,3,4,2,1,0:T(8,128)(2,1)S(1)}, u32[]{:S(2)}, u32[]{:S(2)}) collective-permute-start(bf16[3,1,2,2,1,192,128]{6,5,3,4,2,1,0:T(8,128)(2,1)S(1)} %pad_maximum_fusion.9), channel_id=1, source_target_pairs={{0,2},{2,4},{4,6},{1,3},{3,5},{5,7},{8,10},{10,12},{12,14},{9,11},... | collective-permute-start | bytes 1769480 | tf_op jit(solution)/shard_map/ppermute | solution.py:14
  22.4 1.3 %collective-permute-start.3 = (bf16[3,1,2,2,1,192,128]{6,5,3,4,2,1,0:T(8,128)(2,1)S(1)}, bf16[3,1,2,2,1,192,128]{6,5,3,4,2,1,0:T(8,128)(2,1)S(1)}, u32[]{:S(2)}, u32[]{:S(2)}) collective-permute-start(bf16[3,1,2,2,1,192,128]{6,5,3,4,2,1,0:T(8,128)(2,1)S(1)} %pad_maximum_fusion.9), channel_id=1, source_target_pairs={{2,0},{4,2},{6,4},{3,1},{5,3},{7,5},{10,8},{12,10},{14,12},{11,9},... | collective-permute-start | bytes 1769480 | tf_op jit(solution)/shard_map/ppermute | solution.py:15
  23.7 2.7 %collective-permute-done.2 = bf16[3,1,2,2,1,192,128]{6,5,3,4,2,1,0:T(8,128)(2,1)S(1)} collective-permute-done((bf16[3,1,2,2,1,192,128]{6,5,3,4,2,1,0:T(8,128)(2,1)S(1)}, bf16[3,1,2,2,1,192,128]{6,5,3,4,2,1,0:T(8,128)(2,1)S(1)}, u32[]{:S(2)}, u32[]{:S(2)}) %collective-permute-start.2) | collective-permute-done | bytes 589856 | tf_op jit(solution)/shard_map/ppermute | solution.py:14
  26.5 9.9 %collective-permute-done.3 = bf16[3,1,2,2,1,192,128]{6,5,3,4,2,1,0:T(8,128)(2,1)S(1)} collective-permute-done((bf16[3,1,2,2,1,192,128]{6,5,3,4,2,1,0:T(8,128)(2,1)S(1)}, bf16[3,1,2,2,1,192,128]{6,5,3,4,2,1,0:T(8,128)(2,1)S(1)}, u32[]{:S(2)}, u32[]{:S(2)}) %collective-permute-start.3) | collective-permute-done | bytes 589856 | tf_op jit(solution)/shard_map/ppermute | solution.py:15
  37.4 0.7 copy-done.3
  39.8 1.2 %conditional.31 = (f32[2,1,192,128]{3,2,0,1:T(8,128)S(1)}, bf16[2,2,1,192,128]{4,3,1,2,0:T(8,128)(2,1)S(1)}) conditional(s32[]{:T(128)} %convert_element_type.373, () %tuple.471, (pred[]{:T(512)}, bf16[2,1,192,128]{3,2,0,1:T(8,128)(2,1)S(1)}, bf16[1,1,2,2,1,192,128]{6,5,3,4,2,1,0:T(8,128)(2,1)S(1)}, f32[2,1,192]{2,0,1:T(2,128)S(1)}, ...), branch_computations={%region_45.46_spmd, %region_46.47_spmd} | conditional | flops 95158272 | bytes 2953233 | solution.py:173
  41.1 0.7 copy-done.5
  41.8 0.7 conditional.35
  41.8 0.7 broadcast.1729
  42.5 1.0 %pad_maximum_fusion.10 = bf16[3,2,2,1,192,128]{5,4,2,1,3,0:T(8,128)(2,1)S(1)} fusion(bf16[1,2,2,1,192,128]{5,4,2,1,3,0:T(8,128)(2,1)} %bitcast.185, bf16[1,2,2,1,192,128]{5,4,2,1,3,0:T(8,128)(2,1)S(1)} %bitcast.545, bf16[1,2,2,1,192,128]{5,4,2,1,3,0:T(8,128)(2,1)S(1)} %bitcast.543), kind=kLoop, calls=%fused_computation.291 | loop fusion | flops 589824 | bytes 1179648 | tf_op jit(solution)/shard_map/stack | solution.py:186
  43.5 4.8 %collective-permute-start.4 = (bf16[3,2,2,1,192,128]{5,4,2,1,3,0:T(8,128)(2,1)S(1)}, bf16[3,2,2,1,192,128]{5,4,2,1,3,0:T(8,128)(2,1)S(1)}, u32[]{:S(2)}, u32[]{:S(2)}) collective-permute-start(bf16[3,2,2,1,192,128]{5,4,2,1,3,0:T(8,128)(2,1)S(1)} %pad_maximum_fusion.10), channel_id=1, source_target_pairs={{0,2},{2,4},{4,6},{1,3},{3,5},{5,7},{8,10},{10,12},{12,14},{9,11},... | collective-permute-start | bytes 1769480 | tf_op jit(solution)/shard_map/ppermute | solution.py:23
  48.4 1.4 %collective-permute-start.5 = (bf16[3,2,2,1,192,128]{5,4,2,1,3,0:T(8,128)(2,1)S(1)}, bf16[3,2,2,1,192,128]{5,4,2,1,3,0:T(8,128)(2,1)S(1)}, u32[]{:S(2)}, u32[]{:S(2)}) collective-permute-start(bf16[3,2,2,1,192,128]{5,4,2,1,3,0:T(8,128)(2,1)S(1)} %pad_maximum_fusion.11), channel_id=1, source_target_pairs={{2,0},{4,2},{6,4},{3,1},{5,3},{7,5},{10,8},{12,10},{14,12},{11,9},... | collective-permute-start | bytes 1769480 | tf_op jit(solution)/shard_map/ppermute | solution.py:23
  49.9 10.2 %collective-permute-done.4 = bf16[3,2,2,1,192,128]{5,4,2,1,3,0:T(8,128)(2,1)S(1)} collective-permute-done((bf16[3,2,2,1,192,128]{5,4,2,1,3,0:T(8,128)(2,1)S(1)}, bf16[3,2,2,1,192,128]{5,4,2,1,3,0:T(8,128)(2,1)S(1)}, u32[]{:S(2)}, u32[]{:S(2)}) %collective-permute-start.4) | collective-permute-done | bytes 589856 | tf_op jit(solution)/shard_map/ppermute | solution.py:23
  60.0 7.1 %collective-permute-done.5 = bf16[3,2,2,1,192,128]{5,4,2,1,3,0:T(8,128)(2,1)S(1)} collective-permute-done((bf16[3,2,2,1,192,128]{5,4,2,1,3,0:T(8,128)(2,1)S(1)}, bf16[3,2,2,1,192,128]{5,4,2,1,3,0:T(8,128)(2,1)S(1)}, u32[]{:S(2)}, u32[]{:S(2)}) %collective-permute-start.5) | collective-permute-done | bytes 589856 | tf_op jit(solution)/shard_map/ppermute | solution.py:23
  67.2 1.9 %collective-permute-start.6 = (bf16[2,2,1,192,128]{4,3,1,0,2:T(8,128)(2,1)S(1)}, bf16[2,2,1,192,128]{4,3,1,0,2:T(8,128)(2,1)S(1)}, u32[]{:S(2)}, u32[]{:S(2)}) collective-permute-start(bf16[2,2,1,192,128]{4,3,1,0,2:T(8,128)(2,1)S(1)} %fusion.202), channel_id=1, source_target_pairs={{0,8},{8,16},{16,24},{1,9},{9,17},{17,25},{2,10},{10,18},{18,26},{... | collective-permute-start | bytes 589832 | tf_op jit(solution)/shard_map/ppermute | solution.py:23
  69.2 2.4 %collective-permute-start.7 = (bf16[2,2,1,192,128]{4,3,1,2,0:T(8,128)(2,1)S(1)}, bf16[2,2,1,192,128]{4,3,1,2,0:T(8,128)(2,1)S(1)}, u32[]{:S(2)}, u32[]{:S(2)}) collective-permute-start(bf16[2,2,1,192,128]{4,3,1,2,0:T(8,128)(2,1)S(1)} %fusion.200), channel_id=1, source_target_pairs={{8,0},{16,8},{24,16},{9,1},{17,9},{25,17},{10,2},{18,10},{26,18},{... | collective-permute-start | bytes 589832 | tf_op jit(solution)/shard_map/ppermute | solution.py:23
  71.7 0.7 fusion.208
  72.4 3.8 %collective-permute-done.7 = bf16[2,2,1,192,128]{4,3,1,2,0:T(8,128)(2,1)S(1)} collective-permute-done((bf16[2,2,1,192,128]{4,3,1,2,0:T(8,128)(2,1)S(1)}, bf16[2,2,1,192,128]{4,3,1,2,0:T(8,128)(2,1)S(1)}, u32[]{:S(2)}, u32[]{:S(2)}) %collective-permute-start.7) | collective-permute-done | bytes 196640 | tf_op jit(solution)/shard_map/ppermute | solution.py:23
  76.4 0.7 slice_bitcast_fusion.6
  (87 shorter events, 5.8 us)
Async XLA Ops:
  0.6 12.6 %copy-start.2 = (bf16[1,1,2,1,192,128]{5,4,3,2,1,0:T(8,128)(2,1)S(1)}, bf16[1,1,2,1,192,128]{5,4,3,2,1,0:T(8,128)(2,1)}, u32[]{:S(2)}) copy-start(bf16[1,1,2,1,192,128]{5,4,3,2,1,0:T(8,128)(2,1)} %param.187) | copy-start | bytes 294916
  0.6 12.6 %copy-start.13 = (bf16[1,1,2,1,192,128]{5,4,3,2,1,0:T(8,128)(2,1)S(1)}, bf16[1,1,2,1,192,128]{5,4,3,2,1,0:T(8,128)(2,1)}, u32[]{:S(2)}) copy-start(bf16[1,1,2,1,192,128]{5,4,3,2,1,0:T(8,128)(2,1)} %param.188) | copy-start | bytes 294916
  1.7 7.2 %copy-start.7 = (bf16[1,1,2,2,1,192,128]{6,5,3,4,2,1,0:T(8,128)(2,1)}, bf16[1,1,2,2,1,192,128]{6,5,3,4,2,1,0:T(8,128)(2,1)S(1)}, u32[]{:S(2)}) copy-start(bf16[1,1,2,2,1,192,128]{6,5,3,4,2,1,0:T(8,128)(2,1)S(1)} %pad_maximum_fusion.12) | copy-start | bytes 589828
  1.7 7.1 %collective-permute-start = (bf16[1,1,2,2,1,192,128]{6,5,3,4,2,1,0:T(8,128)(2,1)S(1)}, bf16[1,1,2,2,1,192,128]{6,5,3,4,2,1,0:T(8,128)(2,1)S(1)}, u32[]{:S(2)}, u32[]{:S(2)}) collective-permute-start(bf16[1,1,2,2,1,192,128]{6,5,3,4,2,1,0:T(8,128)(2,1)S(1)} %pad_maximum_fusion.12), channel_id=1, source_target_pairs={{0,8},{8,16},{16,24},{1,9},{9,17},{17,25},{2,10},{10,18},{18,26},{... | collective-permute-start | bytes 589832 | tf_op jit(solution)/shard_map/ppermute | solution.py:14
  6.2 7.0 %collective-permute-start.1 = (bf16[1,1,2,2,1,192,128]{6,5,3,4,2,1,0:T(8,128)(2,1)S(1)}, bf16[1,1,2,2,1,192,128]{6,5,3,4,2,1,0:T(8,128)(2,1)S(1)}, u32[]{:S(2)}, u32[]{:S(2)}) collective-permute-start(bf16[1,1,2,2,1,192,128]{6,5,3,4,2,1,0:T(8,128)(2,1)S(1)} %pad_maximum_fusion.12), channel_id=1, source_target_pairs={{8,0},{16,8},{24,16},{9,1},{17,9},{25,17},{10,2},{18,10},{26,18},{... | collective-permute-start | bytes 589832 | tf_op jit(solution)/shard_map/ppermute | solution.py:15
  13.3 3.3 %copy-start.15 = (s32[1,1,1,27]{3,2,1,0:T(1,128)S(1)}, s32[1,1,1,27]{3,2,1,0:T(1,128)}, u32[]{:S(2)}) copy-start(s32[1,1,1,27]{3,2,1,0:T(1,128)} %param.191) | copy-start | bytes 328
  13.3 13.2 %collective-permute-start.2 = (bf16[3,1,2,2,1,192,128]{6,5,3,4,2,1,0:T(8,128)(2,1)S(1)}, bf16[3,1,2,2,1,192,128]{6,5,3,4,2,1,0:T(8,128)(2,1)S(1)}, u32[]{:S(2)}, u32[]{:S(2)}) collective-permute-start(bf16[3,1,2,2,1,192,128]{6,5,3,4,2,1,0:T(8,128)(2,1)S(1)} %pad_maximum_fusion.9), channel_id=1, source_target_pairs={{0,2},{2,4},{4,6},{1,3},{3,5},{5,7},{8,10},{10,12},{12,14},{9,11},... | collective-permute-start | bytes 1769480 | tf_op jit(solution)/shard_map/ppermute | solution.py:14
  17.2 5.0 %copy-start.14 = (bf16[1,1,2,1,192,128]{5,4,3,2,1,0:T(8,128)(2,1)S(1)}, bf16[1,1,2,1,192,128]{5,4,3,2,1,0:T(8,128)(2,1)}, u32[]{:S(2)}) copy-start(bf16[1,1,2,1,192,128]{5,4,3,2,1,0:T(8,128)(2,1)} %param.190) | copy-start | bytes 294916
  17.2 5.0 %copy-start = (bf16[1,1,2,1,192,128]{5,4,3,2,1,0:T(8,128)(2,1)S(1)}, bf16[1,1,2,1,192,128]{5,4,3,2,1,0:T(8,128)(2,1)}, u32[]{:S(2)}) copy-start(bf16[1,1,2,1,192,128]{5,4,3,2,1,0:T(8,128)(2,1)} %param.189) | copy-start | bytes 294916
  22.4 14.0 %collective-permute-start.3 = (bf16[3,1,2,2,1,192,128]{6,5,3,4,2,1,0:T(8,128)(2,1)S(1)}, bf16[3,1,2,2,1,192,128]{6,5,3,4,2,1,0:T(8,128)(2,1)S(1)}, u32[]{:S(2)}, u32[]{:S(2)}) collective-permute-start(bf16[3,1,2,2,1,192,128]{6,5,3,4,2,1,0:T(8,128)(2,1)S(1)} %pad_maximum_fusion.9), channel_id=1, source_target_pairs={{2,0},{4,2},{6,4},{3,1},{5,3},{7,5},{10,8},{12,10},{14,12},{11,9},... | collective-permute-start | bytes 1769480 | tf_op jit(solution)/shard_map/ppermute | solution.py:15
  23.7 2.7 %copy-start.1 = (bf16[1,1,2,1,192,128]{5,4,3,2,1,0:T(8,128)(2,1)S(1)}, bf16[1,1,2,1,192,128]{5,4,3,2,1,0:T(8,128)(2,1)}, u32[]{:S(2)}) copy-start(bf16[1,1,2,1,192,128]{5,4,3,2,1,0:T(8,128)(2,1)} %param.186) | copy-start | bytes 294916
  37.4 0.7 copy-start.3
  38.1 0.7 copy-start.9
  38.1 1.0 %copy-start.8 = (bf16[1,1,2,2,1,192,128]{6,5,3,4,2,1,0:T(8,128)(2,1)S(1)}, bf16[1,1,2,2,1,192,128]{6,5,3,4,2,1,0:T(8,128)(2,1)}, u32[]{:S(2)}) copy-start(bf16[1,1,2,2,1,192,128]{6,5,3,4,2,1,0:T(8,128)(2,1)} %copy-done.7) | copy-start | bytes 589828
  39.2 0.7 copy-start.11
  41.1 0.7 copy-start.5
  42.5 5.8 %copy-start.4 = (bf16[2,2,1,192,128]{4,3,1,2,0:T(8,128)(2,1)S(1)}, bf16[2,2,1,192,128]{4,3,1,2,0:T(8,128)(2,1)}, u32[]{:S(2)}) copy-start(bf16[2,2,1,192,128]{4,3,1,2,0:T(8,128)(2,1)} %copy-done.3) | copy-start | bytes 589828
  43.5 16.5 %collective-permute-start.4 = (bf16[3,2,2,1,192,128]{5,4,2,1,3,0:T(8,128)(2,1)S(1)}, bf16[3,2,2,1,192,128]{5,4,2,1,3,0:T(8,128)(2,1)S(1)}, u32[]{:S(2)}, u32[]{:S(2)}) collective-permute-start(bf16[3,2,2,1,192,128]{5,4,2,1,3,0:T(8,128)(2,1)S(1)} %pad_maximum_fusion.10), channel_id=1, source_target_pairs={{0,2},{2,4},{4,6},{1,3},{3,5},{5,7},{8,10},{10,12},{12,14},{9,11},... | collective-permute-start | bytes 1769480 | tf_op jit(solution)/shard_map/ppermute | solution.py:23
  48.3 18.8 %copy-start.12 = (bf16[2,2,1,192,128]{4,3,1,2,0:T(8,128)(2,1)S(1)}, bf16[2,2,1,192,128]{4,3,1,2,0:T(8,128)(2,1)}, u32[]{:S(2)}) copy-start(bf16[2,2,1,192,128]{4,3,1,2,0:T(8,128)(2,1)} %copy-done.11) | copy-start | bytes 589828
  48.4 20.7 %copy-start.10 = (bf16[2,2,1,192,128]{4,3,1,2,0:T(8,128)(2,1)S(1)}, bf16[2,2,1,192,128]{4,3,1,2,0:T(8,128)(2,1)}, u32[]{:S(2)}) copy-start(bf16[2,2,1,192,128]{4,3,1,2,0:T(8,128)(2,1)} %copy-done.9) | copy-start | bytes 589828
  48.4 18.7 %collective-permute-start.5 = (bf16[3,2,2,1,192,128]{5,4,2,1,3,0:T(8,128)(2,1)S(1)}, bf16[3,2,2,1,192,128]{5,4,2,1,3,0:T(8,128)(2,1)S(1)}, u32[]{:S(2)}, u32[]{:S(2)}) collective-permute-start(bf16[3,2,2,1,192,128]{5,4,2,1,3,0:T(8,128)(2,1)S(1)} %pad_maximum_fusion.11), channel_id=1, source_target_pairs={{2,0},{4,2},{6,4},{3,1},{5,3},{7,5},{10,8},{12,10},{14,12},{11,9},... | collective-permute-start | bytes 1769480 | tf_op jit(solution)/shard_map/ppermute | solution.py:23
  67.2 5.2 %collective-permute-start.6 = (bf16[2,2,1,192,128]{4,3,1,0,2:T(8,128)(2,1)S(1)}, bf16[2,2,1,192,128]{4,3,1,0,2:T(8,128)(2,1)S(1)}, u32[]{:S(2)}, u32[]{:S(2)}) collective-permute-start(bf16[2,2,1,192,128]{4,3,1,0,2:T(8,128)(2,1)S(1)} %fusion.202), channel_id=1, source_target_pairs={{0,8},{8,16},{16,24},{1,9},{9,17},{17,25},{2,10},{10,18},{18,26},{... | collective-permute-start | bytes 589832 | tf_op jit(solution)/shard_map/ppermute | solution.py:23
  69.2 7.0 %collective-permute-start.7 = (bf16[2,2,1,192,128]{4,3,1,2,0:T(8,128)(2,1)S(1)}, bf16[2,2,1,192,128]{4,3,1,2,0:T(8,128)(2,1)S(1)}, u32[]{:S(2)}, u32[]{:S(2)}) collective-permute-start(bf16[2,2,1,192,128]{4,3,1,2,0:T(8,128)(2,1)S(1)} %fusion.200), channel_id=1, source_target_pairs={{8,0},{16,8},{24,16},{9,1},{17,9},{25,17},{10,2},{18,10},{26,18},{... | collective-permute-start | bytes 589832 | tf_op jit(solution)/shard_map/ppermute | solution.py:23
  71.6 4.6 %copy-start.6 = (bf16[2,2,1,192,128]{4,3,1,2,0:T(8,128)(2,1)S(1)}, bf16[2,2,1,192,128]{4,3,1,2,0:T(8,128)(2,1)}, u32[]{:S(2)}) copy-start(bf16[2,2,1,192,128]{4,3,1,2,0:T(8,128)(2,1)} %copy-done.5) | copy-start | bytes 589828
where the time goes:
time: 77 us
  waiting for transfers between devices  38.7 us (50%)
  starting transfers between devices  21.5 us (28%)
  between operations  6.08 us (8%)
  local copies, waits for them, and re-layouts  5.47 us (7%)
  other arithmetic  3.47 us (5%)
  matrix products  1.43 us (2%)
    ppermute x4, waiting for transfers between devices, from_behind(): return lax.ppermute(block, axis, route)  21.1 us
    ppermute x2, waiting for transfers between devices, with_halo(): after = lax.ppermute(initial, axis, down)  14.3 us
    ppermute x4, starting transfers between devices, from_behind(): return lax.ppermute(block, axis, route)  10.5 us
    ppermute x2, starting transfers between devices, with_halo(): before = lax.ppermute(last, axis, up)  7.78 us
    ppermute x2, waiting for transfers between devices, with_halo(): before = lax.ppermute(last, axis, up)  3.37 us
    ppermute x2, starting transfers between devices, with_halo(): after = lax.ppermute(initial, axis, down)  3.21 us
    unnamed x32, local copies, waits for them, and re-layouts  3.05 us
  transfers between devices with their start and end apart: 8, of which 7 were waited for; matrix products, arithmetic and copies ran while one was open for 2% of the time, Pallas kernels for 0%

commit v1 on v0

v1 whole, which is shorter than its diff:
```python
import functools

import jax
import jax.numpy as jnp
from jax import lax
from jax.experimental import pallas as pl
from jax.experimental.pallas import tpu as pltpu
from jax.sharding import PartitionSpec as P

VMEM = pl.BlockSpec(memory_space=pltpu.VMEM)
SMEM = pl.BlockSpec(memory_space=pltpu.SMEM)
LIMIT = pltpu.CompilerParams(vmem_limit_bytes=32 * 1024 * 1024)
ROWS_T = (((1,), (1,)), ((), ()))
COLS_T = (((0,), (0,)), ((), ()))


def dot(a, b, dims=(((1,), (0,)), ((), ()))):
    return lax.dot_general(a, b, dims, preferred_element_type=jnp.float32)


def place():
    t = lax.axis_index("tm")
    return t // 2, t % 2, lax.axis_index("height")


def flag(mask_ref, dt, dh):
    return (mask_ref[0, 0, 0, 9 * dt + 3 * dh + 1] != 0).astype(jnp.float32)


def pack_kernel(tok, k_ref, v_ref, q_ref, g_ref, o_ref, mask_ref, other_ref, cross_ref, along_ref):
    _, c, _ = place()
    for i, ref in enumerate((k_ref, v_ref, q_ref, g_ref, o_ref)):
        block = ref[0, 0, 1 - c, 0]
        other_ref[pl.ds(i * tok, tok), :] = block
        if i < 2:
            cross_ref[pl.ds(i * tok, tok), :] = block
            along_ref[pl.ds(i * tok, tok), :] = ref[0, 0, c, 0]
    row = lax.broadcasted_iota(jnp.int32, (16, other_ref.shape[1]), 0)
    flags = jnp.zeros(row.shape, jnp.float32)
    for dt in range(3):
        for dh in range(3):
            flags = jnp.where(row == 3 * dt + dh, flag(mask_ref, dt, dh), flags)
    other_ref[pl.ds(5 * tok, 16), :] = flags.astype(jnp.bfloat16)


def line_kernel(tok, chips, own_ref, par_ref, cross_ref, along_ref, line_ref):
    y, c, _ = place()
    for i in range(2):
        rows = pl.ds(i * tok, tok)
        line_ref[i, pl.ds(pl.multiple_of(c * tok, tok), tok), :] = own_ref[rows, :]
        line_ref[i, pl.ds(pl.multiple_of((1 - c) * tok, tok), tok), :] = par_ref[rows, :]
        if chips == 2:
            line_ref[i, pl.ds(2 * tok, tok), :] = jnp.where(
                c != y, cross_ref[rows, :], along_ref[rows, :]
            )
        else:
            line_ref[i, pl.ds(pl.multiple_of((2 + c) * tok, tok), tok), :] = cross_ref[rows, :]
            line_ref[i, pl.ds(pl.multiple_of((3 - c) * tok, tok), tok), :] = along_ref[rows, :]


def main_kernel(
    tok, chips, heights, scale,
    q_ref, g_ref, o_ref, mask_ref, par_ref, here_ref, before_ref, after_ref,
    down_ref, own_ref, up_ref, dq_ref,
    qs, gs, s_ref,
):
    y, c, z = place()
    two = 2 * tok
    slots = here_ref.shape[1] // tok
    mine = pl.ds(pl.multiple_of(c * tok, tok), tok)
    other = pl.ds(pl.multiple_of((1 - c) * tok, tok), tok)
    qs[mine, :] = q_ref[0, 0, c, 0]
    qs[other, :] = par_ref[pl.ds(2 * tok, tok), :]
    gs[mine, :] = g_ref[0, 0, c, 0]
    gs[other, :] = par_ref[pl.ds(3 * tok, tok), :]
    f32 = jnp.float32
    product_own = g_ref[0, 0, c, 0].astype(f32) * o_ref[0, 0, c, 0].astype(f32)
    product_par = par_ref[pl.ds(3 * tok, tok), :].astype(f32) * par_ref[pl.ds(4 * tok, tok), :].astype(f32)
    first = c == 0
    product = jnp.concatenate(
        [jnp.where(first, product_own, product_par), jnp.where(first, product_par, product_own)], axis=0
    )
    delta = jnp.sum(product.T, axis=0, keepdims=True)

    width = par_ref.shape[1]
    lane = lax.broadcasted_iota(jnp.int32, (1, width), 1)
    even, odd = {}, {}
    for dt in range(3):
        for dh in range(3):
            i = 3 * dt + dh
            if i == 4:
                even[i] = odd[i] = jnp.ones((1, width), f32)
                continue
            own = jnp.full((1, width), flag(mask_ref, dt, dh), f32)
            par = par_ref[pl.ds(5 * tok, 16), :].astype(f32)[i : i + 1]
            even[i], odd[i] = jnp.where(first, own, par), jnp.where(first, par, own)
    has_below = (y > 0).astype(f32)
    has_above = (y < chips - 1).astype(f32)
    none = jnp.zeros((1, width), f32)

    def bias(slot, dh):
        e, o = [
            lambda: (even[3 + dh], odd[dh]),
            lambda: (even[6 + dh], odd[3 + dh]),
            lambda: (even[dh] * has_below, odd[6 + dh] * has_above if chips == 2 else none),
            lambda: (none, odd[6 + dh] * has_above),
        ][slot]()
        row = spread(e, o)
        inside = ((z + dh - 1 >= 0) & (z + dh - 1 < heights)).astype(f32)
        return (row * inside - 1.0) * 1e30

    def spread(e, o):
        parts = []
        for start in range(0, two, width):
            parts.append(jnp.where(lane + start < tok, e, o))
        return jnp.concatenate(parts, axis=1)

    sources = (before_ref, here_ref, after_ref)
    blocks = [(dh, slot) for dh in (1, 0, 2) for slot in range(slots)]

    def rows_of(dh, slot):
        return pl.ds((dh * slots + slot) * tok, tok)

    top = jnp.full((8, two), -1e30, f32)
    for dh, slot in blocks:
        keys = sources[dh][0, pl.ds(slot * tok, tok), :]
        scores = dot(keys, qs[...], ROWS_T) * scale + bias(slot, dh)
        s_ref[rows_of(dh, slot), :] = scores
        top = jnp.maximum(top, jnp.max(scores.reshape(tok // 8, 8, two), axis=0))
    top = jnp.max(top, axis=0, keepdims=True)
    total = jnp.zeros((8, two), f32)
    for dh, slot in blocks:
        weights = jnp.exp(s_ref[rows_of(dh, slot), :] - top)
        s_ref[rows_of(dh, slot), :] = weights
        total = total + jnp.sum(weights.reshape(tok // 8, 8, two), axis=0)
    share = 1.0 / jnp.sum(total, axis=0, keepdims=True)

    dq = jnp.zeros((two, width), f32)
    results = (down_ref, own_ref, up_ref)
    for dh, slot in [(dh, slot) for dh in (0, 2, 1) for slot in range(slots)]:
        rows = pl.ds(slot * tok, tok)
        keys = sources[dh][0, rows, :]
        probs = s_ref[rows_of(dh, slot), :] * share
        grads = dot(sources[dh][1, rows, :], gs[...], ROWS_T)
        low = (probs * (grads - delta)).astype(jnp.bfloat16)
        results[dh][0, rows, :] = (dot(low, qs[...]) * scale).astype(jnp.bfloat16)
        results[dh][1, rows, :] = dot(probs.astype(jnp.bfloat16), gs[...]).astype(jnp.bfloat16)
        dq = dq + dot(low, keys, COLS_T)
    dq_ref[...] = (dq * scale).astype(jnp.bfloat16)


def sum_kernel(tok, own_ref, below_ref, above_ref, dq_ref, mine_ref, swap_ref, *halo_refs):
    _, c, _ = place()
    f32 = jnp.float32

    def total(i, start):
        rows = pl.ds(pl.multiple_of(start, tok), tok)
        return own_ref[i, rows, :].astype(f32) + below_ref[i, rows, :].astype(f32) + above_ref[i, rows, :].astype(f32)

    for i in range(2):
        mine_ref[i] = total(i, c * tok)
        swap_ref[i] = total(i, (1 - c) * tok).astype(jnp.bfloat16)
        if len(halo_refs) == 1:
            halo_refs[0][i] = total(i, 2 * tok).astype(jnp.bfloat16)
        else:
            halo_refs[0][i] = total(i, (2 + c) * tok).astype(jnp.bfloat16)
            halo_refs[1][i] = total(i, (3 - c) * tok).astype(jnp.bfloat16)
    swap_ref[2] = dq_ref[pl.ds(pl.multiple_of((1 - c) * tok, tok), tok), :]


def final_kernel(tok, mine_ref, swap_ref, cross_ref, along_ref, dq_ref, gq_ref, gk_ref, gv_ref):
    _, c, _ = place()
    f32 = jnp.float32
    gq_ref[0, 0, c, 0] = dq_ref[pl.ds(pl.multiple_of(c * tok, tok), tok), :]
    gq_ref[0, 0, 1 - c, 0] = swap_ref[2]
    for i, ref in enumerate((gk_ref, gv_ref)):
        ref[0, 0, c, 0] = (mine_ref[i] + along_ref[i].astype(f32)).astype(jnp.bfloat16)
        ref[0, 0, 1 - c, 0] = (swap_ref[i].astype(f32) + cross_ref[i].astype(f32)).astype(jnp.bfloat16)


def body(queries, keys, values, grad_out, attn_out, window_mask):
    tok, width = queries.shape[-2:]
    scale = width ** -0.5
    times, heights = lax.axis_size("tm"), lax.axis_size("height")
    chips = times // 2
    slots = 3 if chips == 2 else 4
    bf16, f32 = jnp.bfloat16, jnp.float32

    def call(kernel, shapes, specs, scratch=(), **kwargs):
        return pl.pallas_call(
            kernel,
            out_shape=[jax.ShapeDtypeStruct(*shape) for shape in shapes],
            in_specs=list(specs),
            out_specs=[VMEM] * len(shapes),
            scratch_shapes=list(scratch),
            compiler_params=LIMIT,
            **kwargs,
        )

    swap = [(t, t ^ 1) for t in range(times)]
    steps = {d: [(t, t + d if t % 2 else t - d) for t in range(times)] for d in (1, 2)}
    cross, along = ([(i, j) for i, j in steps[d] if 0 <= j < times] for d in (1, 2))
    up = [(i, i + 1) for i in range(heights - 1)]
    down = [(j, i) for i, j in up]

    def back(pairs):
        return [(j, i) for i, j in pairs]

    other, near, far = call(
        functools.partial(pack_kernel, tok),
        [((5 * tok + 16, width), bf16), ((2 * tok, width), bf16), ((2 * tok, width), bf16)],
        [VMEM] * 5 + [SMEM],
    )(keys, values, queries, grad_out, attn_out, window_mask)
    near_in = lax.ppermute(near, "tm", cross)
    far_in = lax.ppermute(far, "tm", along)
    par = lax.ppermute(other, "tm", swap)
    (line,) = call(
        functools.partial(line_kernel, tok, chips), [((2, slots * tok, width), bf16)], [VMEM] * 4
    )(far, par, near_in, far_in)
    before = lax.ppermute(line, "height", up)
    after = lax.ppermute(line, "height", down)
    part = ((2, slots * tok, width), bf16)
    to_before, own, to_after, dq = call(
        functools.partial(main_kernel, tok, chips, heights, scale),
        [part, part, part, ((2 * tok, width), bf16)],
        [VMEM] * 3 + [SMEM] + [VMEM] * 4,
        [
            pltpu.VMEM((2 * tok, width), bf16),
            pltpu.VMEM((2 * tok, width), bf16),
            pltpu.VMEM((3 * slots * tok, 2 * tok), f32),
        ],
    )(queries, grad_out, attn_out, window_mask, par, line, before, after)
    from_below = lax.ppermute(to_after, "height", up)
    from_above = lax.ppermute(to_before, "height", down)
    tile = (2, tok, width)
    mine, packed, *halos = call(
        functools.partial(sum_kernel, tok),
        [(tile, f32), ((3, tok, width), bf16)] + [(tile, bf16)] * (slots - 2),
        [VMEM] * 4,
    )(own, from_below, from_above, dq)
    near_back = lax.ppermute(halos[0], "tm", back(cross))
    far_back = lax.ppermute(halos[-1], "tm", back(along))
    swapped = lax.ppermute(packed, "tm", swap)
    return call(
        functools.partial(final_kernel, tok),
        [(queries.shape, bf16)] * 3,
        [VMEM] * 5,
    )(mine, swapped, near_back, far_back, dq)


def solution(mesh):
    placed = P("tm", "height", "dp", None, None, None)
    return jax.shard_map(
        body,
        mesh=mesh,
        in_specs=(placed,) * 5 + (P("tm", "height", None, None),),
        out_specs=(placed,) * 3,
        check_vma=False,
    )
```

time: 77 us -> 53.9 us (0.70)
  waiting for transfers between devices: 38.7 us -> 14.6 us
  starting transfers between devices: 21.5 us -> 27.8 us
  between operations: 6.08 us -> 0.76 us
  Pallas kernels: 0 us -> 5.18 us
  other arithmetic: 3.47 us -> 0 us
  matrix products: 1.43 us -> 0 us
    ppermute x8 -> x10, waiting for transfers between devices: 38.7 us -> 14.6 us  [the longest x1 3.83 us: body(): from_above = lax.ppermute(to_before, 'height', down)]
    ppermute x8 -> x10, starting transfers between devices: 21.5 us -> 27.8 us  [the longest x1 5.6 us: body(): near_back = lax.ppermute(halos[0], 'tm', back(cross))]
    pallas_call x0 -> x5, Pallas kernels: none -> 5.18 us  [the longest x1 3.7 us: body(): call(functools.partial(main_kernel, tok, chips, heights, scale), [part, p...]
    another operation x5 -> x0, other arithmetic: 2.25 us -> none  [the longest x2 1.1 us: body(): jnp.stack([columns[step_time][picked_side] for step_time in range(3)])]
    unnamed x32 -> x18, local copies, waits for them, and re-layouts: 3.05 us -> 5.13 us
    dot_general x6 -> x0, matrix products: 1.43 us -> none  [the longest x2 0.49 us: tile_scores(): jnp.einsum('hwqd,hwkd->hwqk', query_rows, key_rows, preferred_element_typ...]
    another operation x16 -> x0, local copies, waits for them, and re-layouts: 1.02 us -> none
  transfers between devices with their start and end apart: 8 -> 10, of which waited for: 7 -> 8; matrix products, arithmetic and copies ran while one was open for 2% -> 0% of each run, Pallas kernels for 0% -> 0%
where the time goes in v1:
time: 53.9 us; the launch traced here: 53.5 us
  starting transfers between devices  27.8 us (52%)
  waiting for transfers between devices  14.6 us (27%)
  Pallas kernels  5.18 us (10%)
  local copies, waits for them, and re-layouts  5.13 us (10%)
  between operations  0.76 us (1%)
    ppermute x1, starting transfers between devices, body(): near_back = lax.ppermute(halos[0], 'tm', back(cross))  5.6 us
    unnamed x18, local copies, waits for them, and re-layouts  5.13 us
    ppermute x1, starting transfers between devices, body(): near_in = lax.ppermute(near, 'tm', cross)  4.49 us
    ppermute x1, starting transfers between devices, body(): swapped = lax.ppermute(packed, 'tm', swap)  4.2 us
    ppermute x1, starting transfers between devices, body(): from_below = lax.ppermute(to_after, 'height', up)  4.13 us
    ppermute x1, starting transfers between devices, body(): before = lax.ppermute(line, 'height', up)  4 us
    ppermute x1, waiting for transfers between devices, body(): from_above = lax.ppermute(to_before, 'height', down)  3.83 us
    pallas_call x1, Pallas kernels, body(): call(functools.partial(main_kernel, tok, chips, heights, scale), [part, p...  3.7 us
  transfers between devices with their start and end apart: 10, of which 8 were waited for; matrix products, arithmetic and copies ran while one was open for 0% of the time, Pallas kernels for 0%

profile of v1, /device:TPU:1, one launch (start us, length us, event | category | flops | bytes accessed | tf_op | source)
XLA Modules:
  0.0 53.5 jit_solution(13044450571364348141)
XLA Ops:
  0.6 0.9 %copy-done = bf16[1,1,2,1,192,128]{5,4,3,2,1,0:T(8,128)(2,1)S(1)} copy-done((bf16[1,1,2,1,192,128]{5,4,3,2,1,0:T(8,128)(2,1)S(1)}, bf16[1,1,2,1,192,128]{5,4,3,2,1,0:T(8,128)(2,1)}, u32[]{:S(2)}) %copy-start) | copy-done | bytes 98328
  1.5 0.9 %copy-done.2 = bf16[1,1,2,1,192,128]{5,4,3,2,1,0:T(8,128)(2,1)S(1)} copy-done((bf16[1,1,2,1,192,128]{5,4,3,2,1,0:T(8,128)(2,1)S(1)}, bf16[1,1,2,1,192,128]{5,4,3,2,1,0:T(8,128)(2,1)}, u32[]{:S(2)}) %copy-start.2) | copy-done | bytes 98328
  2.4 0.9 %copy-done.4 = bf16[1,1,2,1,192,128]{5,4,3,2,1,0:T(8,128)(2,1)S(1)} copy-done((bf16[1,1,2,1,192,128]{5,4,3,2,1,0:T(8,128)(2,1)S(1)}, bf16[1,1,2,1,192,128]{5,4,3,2,1,0:T(8,128)(2,1)}, u32[]{:S(2)}) %copy-start.4) | copy-done | bytes 98328
  3.3 0.9 %copy-done.6 = bf16[1,1,2,1,192,128]{5,4,3,2,1,0:T(8,128)(2,1)S(1)} copy-done((bf16[1,1,2,1,192,128]{5,4,3,2,1,0:T(8,128)(2,1)S(1)}, bf16[1,1,2,1,192,128]{5,4,3,2,1,0:T(8,128)(2,1)}, u32[]{:S(2)}) %copy-start.6) | copy-done | bytes 98328
  4.2 0.9 %copy-done.7 = bf16[1,1,2,1,192,128]{5,4,3,2,1,0:T(8,128)(2,1)S(1)} copy-done((bf16[1,1,2,1,192,128]{5,4,3,2,1,0:T(8,128)(2,1)S(1)}, bf16[1,1,2,1,192,128]{5,4,3,2,1,0:T(8,128)(2,1)}, u32[]{:S(2)}) %copy-start.7) | copy-done | bytes 98328
  5.1 0.7 %copy-done.8 = s32[1,1,1,27]{3,2,1,0:T(1,128)S(1)} copy-done((s32[1,1,1,27]{3,2,1,0:T(1,128)S(1)}, s32[1,1,1,27]{3,2,1,0:T(1,128)}, u32[]{:S(2)}) %copy-start.8) | copy-done | bytes 132
  6.5 4.5 %collective-permute-start.1 = (bf16[384,128]{1,0:T(8,128)(2,1)S(1)}, bf16[384,128]{1,0:T(8,128)(2,1)S(1)}, u32[]{:S(2)}, u32[]{:S(2)}) collective-permute-start(bf16[384,128]{1,0:T(8,128)(2,1)S(1)} %get-tuple-element.15), channel_id=1, source_target_pairs={{8,16},{16,8},{9,17},{17,9},{10,18},{18,10},{11,19},{19,11},{12,20... | collective-permute-start | bytes 294920 | tf_op jit(solution)/shard_map/ppermute | solution.py:214
  11.0 1.4 %collective-permute-start.2 = (bf16[384,128]{1,0:T(8,128)(2,1)S(1)}, bf16[384,128]{1,0:T(8,128)(2,1)S(1)}, u32[]{:S(2)}, u32[]{:S(2)}) collective-permute-start(bf16[384,128]{1,0:T(8,128)(2,1)S(1)} %get-tuple-element.14.own_ref), channel_id=1, source_target_pairs={{8,24},{16,0},{9,25},{17,1},{10,26},{18,2},{11,27},{19,3},{12,28},... | collective-permute-start | bytes 294920 | tf_op jit(solution)/shard_map/ppermute | solution.py:215
  12.5 0.8 %collective-permute-done.1.cross_ref = bf16[384,128]{1,0:T(8,128)(2,1)S(1)} collective-permute-done((bf16[384,128]{1,0:T(8,128)(2,1)S(1)}, bf16[384,128]{1,0:T(8,128)(2,1)S(1)}, u32[]{:S(2)}, u32[]{:S(2)}) %collective-permute-start.1) | collective-permute-done | bytes 98336 | tf_op jit(solution)/shard_map/ppermute | solution.py:214
  13.3 0.8 %collective-permute-done.2.along_ref = bf16[384,128]{1,0:T(8,128)(2,1)S(1)} collective-permute-done((bf16[384,128]{1,0:T(8,128)(2,1)S(1)}, bf16[384,128]{1,0:T(8,128)(2,1)S(1)}, u32[]{:S(2)}, u32[]{:S(2)}) %collective-permute-start.2) | collective-permute-done | bytes 98336 | tf_op jit(solution)/shard_map/ppermute | solution.py:215
  14.1 1.3 %collective-permute-start.4 = (bf16[2,576,128]{2,1,0:T(8,128)(2,1)S(1)}, bf16[2,576,128]{2,1,0:T(8,128)(2,1)S(1)}, u32[]{:S(2)}, u32[]{:S(2)}) collective-permute-start(bf16[2,576,128]{2,1,0:T(8,128)(2,1)S(1)} %shard_map.86.here_ref), channel_id=1, source_target_pairs={{2,0},{4,2},{6,4},{3,1},{5,3},{7,5},{10,8},{12,10},{14,12},{11,9},... | collective-permute-start | bytes 884744 | tf_op jit(solution)/shard_map/ppermute | solution.py:221
  15.4 4.0 %collective-permute-start.3 = (bf16[2,576,128]{2,1,0:T(8,128)(2,1)S(1)}, bf16[2,576,128]{2,1,0:T(8,128)(2,1)S(1)}, u32[]{:S(2)}, u32[]{:S(2)}) collective-permute-start(bf16[2,576,128]{2,1,0:T(8,128)(2,1)S(1)} %shard_map.86.here_ref), channel_id=1, source_target_pairs={{0,2},{2,4},{4,6},{1,3},{3,5},{5,7},{8,10},{10,12},{12,14},{9,11},... | collective-permute-start | bytes 884744 | tf_op jit(solution)/shard_map/ppermute | solution.py:220
  19.4 3.6 %collective-permute-done.4.after_ref = bf16[2,576,128]{2,1,0:T(8,128)(2,1)S(1)} collective-permute-done((bf16[2,576,128]{2,1,0:T(8,128)(2,1)S(1)}, bf16[2,576,128]{2,1,0:T(8,128)(2,1)S(1)}, u32[]{:S(2)}, u32[]{:S(2)}) %collective-permute-start.4) | collective-permute-done | bytes 294944 | tf_op jit(solution)/shard_map/ppermute | solution.py:221
  23.0 0.9 %collective-permute-done.3.before_ref = bf16[2,576,128]{2,1,0:T(8,128)(2,1)S(1)} collective-permute-done((bf16[2,576,128]{2,1,0:T(8,128)(2,1)S(1)}, bf16[2,576,128]{2,1,0:T(8,128)(2,1)S(1)}, u32[]{:S(2)}, u32[]{:S(2)}) %collective-permute-start.3) | collective-permute-done | bytes 294944 | tf_op jit(solution)/shard_map/ppermute | solution.py:220
  23.9 3.7 %shard_map.87 = (bf16[2,576,128]{2,1,0:T(8,128)(2,1)S(1)}, bf16[2,576,128]{2,1,0:T(8,128)(2,1)S(1)}, bf16[2,576,128]{2,1,0:T(8,128)(2,1)S(1)}, bf16[384,128]{1,0:T(8,128)(2,1)S(1)}) custom-call(bf16[1,1,2,1,192,128]{5,4,3,2,1,0:T(8,128)(2,1)S(1)} %copy-done.1, bf16[1,1,2,1,192,128]{5,4,3,2,1,0:T(8,128)(2,1)S(1)} %copy-done.3, ...), custom_call_target="tpu_custom_call" | custom-call | tf_op jit(solution)/shard_map/pallas_call | solution.py:223
  27.6 4.1 %collective-permute-start.5 = (bf16[2,576,128]{2,1,0:T(8,128)(2,1)S(1)}, bf16[2,576,128]{2,1,0:T(8,128)(2,1)S(1)}, u32[]{:S(2)}, u32[]{:S(2)}) collective-permute-start(bf16[2,576,128]{2,1,0:T(8,128)(2,1)S(1)} %get-tuple-element.17), channel_id=1, source_target_pairs={{0,2},{2,4},{4,6},{1,3},{3,5},{5,7},{8,10},{10,12},{12,14},{9,11},... | collective-permute-start | bytes 884744 | tf_op jit(solution)/shard_map/ppermute | solution.py:233
  31.8 1.3 %collective-permute-start.6 = (bf16[2,576,128]{2,1,0:T(8,128)(2,1)S(1)}, bf16[2,576,128]{2,1,0:T(8,128)(2,1)S(1)}, u32[]{:S(2)}, u32[]{:S(2)}) collective-permute-start(bf16[2,576,128]{2,1,0:T(8,128)(2,1)S(1)} %get-tuple-element.18), channel_id=1, source_target_pairs={{2,0},{4,2},{6,4},{3,1},{5,3},{7,5},{10,8},{12,10},{14,12},{11,9},... | collective-permute-start | bytes 884744 | tf_op jit(solution)/shard_map/ppermute | solution.py:234
  33.1 2.3 %collective-permute-done.5.below_ref = bf16[2,576,128]{2,1,0:T(8,128)(2,1)S(1)} collective-permute-done((bf16[2,576,128]{2,1,0:T(8,128)(2,1)S(1)}, bf16[2,576,128]{2,1,0:T(8,128)(2,1)S(1)}, u32[]{:S(2)}, u32[]{:S(2)}) %collective-permute-start.5) | collective-permute-done | bytes 294944 | tf_op jit(solution)/shard_map/ppermute | solution.py:233
  35.4 3.8 %collective-permute-done.6.above_ref = bf16[2,576,128]{2,1,0:T(8,128)(2,1)S(1)} collective-permute-done((bf16[2,576,128]{2,1,0:T(8,128)(2,1)S(1)}, bf16[2,576,128]{2,1,0:T(8,128)(2,1)S(1)}, u32[]{:S(2)}, u32[]{:S(2)}) %collective-permute-start.6) | collective-permute-done | bytes 294944 | tf_op jit(solution)/shard_map/ppermute | solution.py:234
  39.3 4.2 %collective-permute-start.7 = (bf16[3,192,128]{2,1,0:T(8,128)(2,1)S(1)}, bf16[3,192,128]{2,1,0:T(8,128)(2,1)S(1)}, u32[]{:S(2)}, u32[]{:S(2)}) collective-permute-start(bf16[3,192,128]{2,1,0:T(8,128)(2,1)S(1)} %get-tuple-element.21), channel_id=1, source_target_pairs={{0,8},{8,0},{16,24},{24,16},{1,9},{9,1},{17,25},{25,17},{2,10},{10... | collective-permute-start | bytes 442376 | tf_op jit(solution)/shard_map/ppermute | solution.py:243
  43.5 1.3 %collective-permute-start.9 = (bf16[2,192,128]{2,1,0:T(8,128)(2,1)S(1)}, bf16[2,192,128]{2,1,0:T(8,128)(2,1)S(1)}, u32[]{:S(2)}, u32[]{:S(2)}) collective-permute-start(bf16[2,192,128]{2,1,0:T(8,128)(2,1)S(1)} %get-tuple-element.22), channel_id=1, source_target_pairs={{24,8},{0,16},{25,9},{1,17},{26,10},{2,18},{27,11},{3,19},{28,12},... | collective-permute-start | bytes 294920 | tf_op jit(solution)/shard_map/ppermute | solution.py:242
  44.8 5.6 %collective-permute-start.8 = (bf16[2,192,128]{2,1,0:T(8,128)(2,1)S(1)}, bf16[2,192,128]{2,1,0:T(8,128)(2,1)S(1)}, u32[]{:S(2)}, u32[]{:S(2)}) collective-permute-start(bf16[2,192,128]{2,1,0:T(8,128)(2,1)S(1)} %get-tuple-element.22), channel_id=1, source_target_pairs={{16,8},{8,16},{17,9},{9,17},{18,10},{10,18},{19,11},{11,19},{20,12... | collective-permute-start | bytes 294920 | tf_op jit(solution)/shard_map/ppermute | solution.py:241
  50.6 2.1 %collective-permute-done.8.cross_ref = bf16[2,192,128]{2,1,0:T(8,128)(2,1)S(1)} collective-permute-done((bf16[2,192,128]{2,1,0:T(8,128)(2,1)S(1)}, bf16[2,192,128]{2,1,0:T(8,128)(2,1)S(1)}, u32[]{:S(2)}, u32[]{:S(2)}) %collective-permute-start.8) | collective-permute-done | bytes 98336 | tf_op jit(solution)/shard_map/ppermute | solution.py:241
  52.7 0.7 %shard_map.89 = (bf16[1,1,2,1,192,128]{5,4,3,2,1,0:T(8,128)(2,1)}, bf16[1,1,2,1,192,128]{5,4,3,2,1,0:T(8,128)(2,1)}, bf16[1,1,2,1,192,128]{5,4,3,2,1,0:T(8,128)(2,1)}) custom-call(f32[2,192,128]{2,1,0:T(8,128)S(1)} %get-tuple-element.20.mine_ref, bf16[3,192,128]{2,1,0:T(8,128)(2,1)S(1)} %collective-permute-done.7.swap_ref, ...), custom_call_target="tpu_custom_call" | custom-call | tf_op jit(solution)/shard_map/pallas_call | solution.py:244
  (19 shorter events, 1.1 us)
Async XLA Ops:
  0.6 0.9 %copy-start = (bf16[1,1,2,1,192,128]{5,4,3,2,1,0:T(8,128)(2,1)S(1)}, bf16[1,1,2,1,192,128]{5,4,3,2,1,0:T(8,128)(2,1)}, u32[]{:S(2)}) copy-start(bf16[1,1,2,1,192,128]{5,4,3,2,1,0:T(8,128)(2,1)} %q_ref.3) | copy-start | bytes 294916
  1.5 0.9 %copy-start.2 = (bf16[1,1,2,1,192,128]{5,4,3,2,1,0:T(8,128)(2,1)S(1)}, bf16[1,1,2,1,192,128]{5,4,3,2,1,0:T(8,128)(2,1)}, u32[]{:S(2)}) copy-start(bf16[1,1,2,1,192,128]{5,4,3,2,1,0:T(8,128)(2,1)} %g_ref.3) | copy-start | bytes 294916
  2.4 0.9 %copy-start.4 = (bf16[1,1,2,1,192,128]{5,4,3,2,1,0:T(8,128)(2,1)S(1)}, bf16[1,1,2,1,192,128]{5,4,3,2,1,0:T(8,128)(2,1)}, u32[]{:S(2)}) copy-start(bf16[1,1,2,1,192,128]{5,4,3,2,1,0:T(8,128)(2,1)} %o_ref.3) | copy-start | bytes 294916
  3.3 0.9 %copy-start.6 = (bf16[1,1,2,1,192,128]{5,4,3,2,1,0:T(8,128)(2,1)S(1)}, bf16[1,1,2,1,192,128]{5,4,3,2,1,0:T(8,128)(2,1)}, u32[]{:S(2)}) copy-start(bf16[1,1,2,1,192,128]{5,4,3,2,1,0:T(8,128)(2,1)} %k_ref.1) | copy-start | bytes 294916
  4.2 0.9 %copy-start.7 = (bf16[1,1,2,1,192,128]{5,4,3,2,1,0:T(8,128)(2,1)S(1)}, bf16[1,1,2,1,192,128]{5,4,3,2,1,0:T(8,128)(2,1)}, u32[]{:S(2)}) copy-start(bf16[1,1,2,1,192,128]{5,4,3,2,1,0:T(8,128)(2,1)} %v_ref.1) | copy-start | bytes 294916
  5.1 0.7 %copy-start.8 = (s32[1,1,1,27]{3,2,1,0:T(1,128)S(1)}, s32[1,1,1,27]{3,2,1,0:T(1,128)}, u32[]{:S(2)}) copy-start(s32[1,1,1,27]{3,2,1,0:T(1,128)} %mask_ref.3) | copy-start | bytes 328
  6.4 7.7 %collective-permute-start = (bf16[976,128]{1,0:T(8,128)(2,1)S(1)}, bf16[976,128]{1,0:T(8,128)(2,1)S(1)}, u32[]{:S(2)}, u32[]{:S(2)}) collective-permute-start(bf16[976,128]{1,0:T(8,128)(2,1)S(1)} %get-tuple-element.13), channel_id=1, source_target_pairs={{0,8},{8,0},{16,24},{24,16},{1,9},{9,1},{17,25},{25,17},{2,10},{10... | collective-permute-start | bytes 749576 | tf_op jit(solution)/shard_map/ppermute | solution.py:216
  6.5 6.8 %collective-permute-start.1 = (bf16[384,128]{1,0:T(8,128)(2,1)S(1)}, bf16[384,128]{1,0:T(8,128)(2,1)S(1)}, u32[]{:S(2)}, u32[]{:S(2)}) collective-permute-start(bf16[384,128]{1,0:T(8,128)(2,1)S(1)} %get-tuple-element.15), channel_id=1, source_target_pairs={{8,16},{16,8},{9,17},{17,9},{10,18},{18,10},{11,19},{19,11},{12,20... | collective-permute-start | bytes 294920 | tf_op jit(solution)/shard_map/ppermute | solution.py:214
  11.0 12.9 %copy-start.1 = (bf16[1,1,2,1,192,128]{5,4,3,2,1,0:T(8,128)(2,1)S(1)}, bf16[1,1,2,1,192,128]{5,4,3,2,1,0:T(8,128)(2,1)}, u32[]{:S(2)}) copy-start(bf16[1,1,2,1,192,128]{5,4,3,2,1,0:T(8,128)(2,1)} %q_ref.3) | copy-start | bytes 294916
  11.0 12.9 %copy-start.3 = (bf16[1,1,2,1,192,128]{5,4,3,2,1,0:T(8,128)(2,1)S(1)}, bf16[1,1,2,1,192,128]{5,4,3,2,1,0:T(8,128)(2,1)}, u32[]{:S(2)}) copy-start(bf16[1,1,2,1,192,128]{5,4,3,2,1,0:T(8,128)(2,1)} %g_ref.3) | copy-start | bytes 294916
  11.0 12.9 %copy-start.5 = (bf16[1,1,2,1,192,128]{5,4,3,2,1,0:T(8,128)(2,1)S(1)}, bf16[1,1,2,1,192,128]{5,4,3,2,1,0:T(8,128)(2,1)}, u32[]{:S(2)}) copy-start(bf16[1,1,2,1,192,128]{5,4,3,2,1,0:T(8,128)(2,1)} %o_ref.3) | copy-start | bytes 294916
  11.0 3.1 %collective-permute-start.2 = (bf16[384,128]{1,0:T(8,128)(2,1)S(1)}, bf16[384,128]{1,0:T(8,128)(2,1)S(1)}, u32[]{:S(2)}, u32[]{:S(2)}) collective-permute-start(bf16[384,128]{1,0:T(8,128)(2,1)S(1)} %get-tuple-element.14.own_ref), channel_id=1, source_target_pairs={{8,24},{16,0},{9,25},{17,1},{10,26},{18,2},{11,27},{19,3},{12,28},... | collective-permute-start | bytes 294920 | tf_op jit(solution)/shard_map/ppermute | solution.py:215
  14.1 8.9 %collective-permute-start.4 = (bf16[2,576,128]{2,1,0:T(8,128)(2,1)S(1)}, bf16[2,576,128]{2,1,0:T(8,128)(2,1)S(1)}, u32[]{:S(2)}, u32[]{:S(2)}) collective-permute-start(bf16[2,576,128]{2,1,0:T(8,128)(2,1)S(1)} %shard_map.86.here_ref), channel_id=1, source_target_pairs={{2,0},{4,2},{6,4},{3,1},{5,3},{7,5},{10,8},{12,10},{14,12},{11,9},... | collective-permute-start | bytes 884744 | tf_op jit(solution)/shard_map/ppermute | solution.py:221
  15.4 8.5 %collective-permute-start.3 = (bf16[2,576,128]{2,1,0:T(8,128)(2,1)S(1)}, bf16[2,576,128]{2,1,0:T(8,128)(2,1)S(1)}, u32[]{:S(2)}, u32[]{:S(2)}) collective-permute-start(bf16[2,576,128]{2,1,0:T(8,128)(2,1)S(1)} %shard_map.86.here_ref), channel_id=1, source_target_pairs={{0,2},{2,4},{4,6},{1,3},{3,5},{5,7},{8,10},{10,12},{12,14},{9,11},... | collective-permute-start | bytes 884744 | tf_op jit(solution)/shard_map/ppermute | solution.py:220
  27.6 7.8 %collective-permute-start.5 = (bf16[2,576,128]{2,1,0:T(8,128)(2,1)S(1)}, bf16[2,576,128]{2,1,0:T(8,128)(2,1)S(1)}, u32[]{:S(2)}, u32[]{:S(2)}) collective-permute-start(bf16[2,576,128]{2,1,0:T(8,128)(2,1)S(1)} %get-tuple-element.17), channel_id=1, source_target_pairs={{0,2},{2,4},{4,6},{1,3},{3,5},{5,7},{8,10},{10,12},{12,14},{9,11},... | collective-permute-start | bytes 884744 | tf_op jit(solution)/shard_map/ppermute | solution.py:233
  31.8 7.5 %collective-permute-start.6 = (bf16[2,576,128]{2,1,0:T(8,128)(2,1)S(1)}, bf16[2,576,128]{2,1,0:T(8,128)(2,1)S(1)}, u32[]{:S(2)}, u32[]{:S(2)}) collective-permute-start(bf16[2,576,128]{2,1,0:T(8,128)(2,1)S(1)} %get-tuple-element.18), channel_id=1, source_target_pairs={{2,0},{4,2},{6,4},{3,1},{5,3},{7,5},{10,8},{12,10},{14,12},{11,9},... | collective-permute-start | bytes 884744 | tf_op jit(solution)/shard_map/ppermute | solution.py:234
  39.3 13.4 %collective-permute-start.7 = (bf16[3,192,128]{2,1,0:T(8,128)(2,1)S(1)}, bf16[3,192,128]{2,1,0:T(8,128)(2,1)S(1)}, u32[]{:S(2)}, u32[]{:S(2)}) collective-permute-start(bf16[3,192,128]{2,1,0:T(8,128)(2,1)S(1)} %get-tuple-element.21), channel_id=1, source_target_pairs={{0,8},{8,0},{16,24},{24,16},{1,9},{9,1},{17,25},{25,17},{2,10},{10... | collective-permute-start | bytes 442376 | tf_op jit(solution)/shard_map/ppermute | solution.py:243
  43.5 7.1 %collective-permute-start.9 = (bf16[2,192,128]{2,1,0:T(8,128)(2,1)S(1)}, bf16[2,192,128]{2,1,0:T(8,128)(2,1)S(1)}, u32[]{:S(2)}, u32[]{:S(2)}) collective-permute-start(bf16[2,192,128]{2,1,0:T(8,128)(2,1)S(1)} %get-tuple-element.22), channel_id=1, source_target_pairs={{24,8},{0,16},{25,9},{1,17},{26,10},{2,18},{27,11},{3,19},{28,12},... | collective-permute-start | bytes 294920 | tf_op jit(solution)/shard_map/ppermute | solution.py:242
  44.8 7.9 %collective-permute-start.8 = (bf16[2,192,128]{2,1,0:T(8,128)(2,1)S(1)}, bf16[2,192,128]{2,1,0:T(8,128)(2,1)S(1)}, u32[]{:S(2)}, u32[]{:S(2)}) collective-permute-start(bf16[2,192,128]{2,1,0:T(8,128)(2,1)S(1)} %get-tuple-element.22), channel_id=1, source_target_pairs={{16,8},{8,16},{17,9},{9,17},{18,10},{10,18},{19,11},{11,19},{20,12... | collective-permute-start | bytes 294920 | tf_op jit(solution)/shard_map/ppermute | solution.py:241
